TPU v7x, 256 devices: a whole 4x4x8 slice. The times are simulated.
256 devices in a mesh: leaf: 32 (over z, y), front: 8 (over x, core).
Axes of the slice: x: 4, y: 4, z: 8, core: 2. Of those that a mesh axis runs over, the one named last changes fastest.
Arguments:
- leaf_fronts: float32 [32, 1024, 1024], P('leaf', 'front')
- coupling_cols: int32 [32, 8, 124, 128], P('leaf', 'front'), may hold values from 0 to 1023, as said below
- coupling_vals: float32 [32, 8, 124, 128], P('leaf', 'front'), may hold values from -0.1 to 0.1
- sep_diag: float32 [32, 8, 124], P('leaf', 'front'), may hold values from 1 to 3
- child_maps: int32 [62, 512], replicated, may hold values from 0 to 1023, as said below
Outputs:
- factors: float32 [32, 8, 252, 512], P('leaf', 'front')
- log_det: float32 [], replicated
Inputs may be any that keep to these rules, and one draw needn't show every extreme that they name: `coupling_cols`: each coupling column is at most the index, in its front, of the row that holds it, so every entry lies on or below the diagonal. `child_maps`: the 512 entries of each row are distinct.
All inputs are finite; a program needn't handle non-finite values.
Results may differ from a plain program's by a relative error of at most 0.0001.
Values sent between devices are 32-bit elements; how exact they have to be, the bound alone decides.
A program may use at most 128 MiB of HBM per device.

v0:
```python
import jax
import jax.numpy as jnp
from jax import lax
from jax.sharding import PartitionSpec as P

SEP = 512
BND = 512


highest_precision = lax.Precision.HIGHEST


def swapped(block, axis, distance):
    count = lax.axis_size(axis)
    route = []
    for low in range(count):
        high = low | 1 << distance
        if high != low and high < count:
            route += [(low, high), (high, low)]
    return lax.ppermute(block, axis, route)


def from_behind(block, axis, distance):
    devices = range(lax.axis_size(axis))
    route = [(i - distance, i) for i in devices if i - distance in devices]
    return lax.ppermute(block, axis, route)


def symmetric_of(lower_tri):
    return lower_tri + lower_tri.T - jnp.diag(jnp.diag(lower_tri))


def double_up(gathered, partner, bit_pos):
    leaf_pos = lax.axis_index("leaf")
    high_side = leaf_pos >> bit_pos & 1 == 1
    first_half = jnp.where(high_side, partner, gathered)
    second_half = jnp.where(high_side, gathered, partner)
    return jnp.concatenate([first_half, second_half], axis=0)


def collect(strip_piece, bit_count, is_panel):
    if is_panel:
        gathered = lax.all_gather(strip_piece, "front", axis=0, tiled=True)
    else:
        gathered = lax.all_gather(strip_piece, "front", axis=0, tiled=True)
    for bit_pos in range(bit_count):
        if is_panel:
            partner = swapped(gathered, "leaf", bit_pos)
        else:
            partner = swapped(gathered, "leaf", bit_pos)
        gathered = double_up(gathered, partner, bit_pos)
    return gathered


def twin_order(gathered, group_size):
    row_count = gathered.shape[0] // (2 * group_size)
    col_count = gathered.shape[1]
    arranged = gathered.reshape(2, 2, group_size // 2, row_count, col_count)
    return arranged.transpose(0, 2, 1, 3, 4).reshape(2, group_size * row_count, col_count)


def child_rows(update_rows, index_map, row_ids):
    match_grid = index_map[None, :] == row_ids[:, None]
    child_ids = jnp.arange(index_map.shape[0], dtype=jnp.int32)
    present = jnp.any(match_grid, axis=1)
    source = jnp.sum(jnp.where(match_grid, child_ids[None, :], 0), axis=1)
    row_part = jnp.take(update_rows, source, axis=0)
    col_part = jnp.take(update_rows, source, axis=1).T
    picked = jnp.where(child_ids[None, :] <= source[:, None], row_part, col_part)
    return jnp.where(present[:, None], picked, 0.0)


def body(leaf_fronts, coupling_cols, coupling_vals, sep_diag, child_maps):
    group_count = lax.axis_size("leaf")
    front_count = lax.axis_size("front")
    level_total = group_count.bit_length()
    width_all = SEP + BND
    leaf_pos = lax.axis_index("leaf")
    front_pos = lax.axis_index("front")
    size_rows = width_all // front_count
    row_ids = front_pos * size_rows + jnp.arange(size_rows, dtype=jnp.int32)
    column_ids = jnp.arange(width_all, dtype=jnp.int32)
    front_strip = jnp.where(column_ids[None, :] <= row_ids[:, None], leaf_fronts[0], 0.0)
    pieces_out = []
    log_part = jnp.zeros((), jnp.float32)
    list_offset = 0
    map_base = 0
    for level_no in range(level_total):
        span_leaf = 1 << level_no
        size_rows = width_all // (front_count * span_leaf)
        group_rank = (leaf_pos & span_leaf - 1) * front_count + front_pos
        start_row = group_rank * size_rows
        panel_piece = front_strip[:, :SEP]
        panel_cols = collect(panel_piece, level_no, True)
        head_block = symmetric_of(panel_cols[:SEP])
        chol_head = jnp.linalg.cholesky(head_block)
        below = jax.scipy.linalg.solve_triangular(chol_head, panel_cols[SEP:].T, lower=True).T
        factor_cols = jnp.concatenate([chol_head, below], axis=0)
        pieces_out.append(lax.dynamic_slice_in_dim(factor_cols, start_row, size_rows, 0))
        head_diag = jnp.diagonal(chol_head)
        owned_rows = jnp.arange(SEP, dtype=jnp.int32) // size_rows == group_rank
        log_part = log_part + jnp.sum(jnp.where(owned_rows, jnp.log(head_diag), 0.0))
        if level_no + 1 < level_total:
            group_size = span_leaf * front_count
            half_rows = size_rows // 2
            holds_tail = group_rank >= group_size // 2
            update_start = start_row - jnp.where(holds_tail, SEP, 0)
            tail_rows = front_strip[:, SEP:]

            def tail_term():
                own_below = lax.dynamic_slice_in_dim(
                    below, jnp.clip(update_start, 0, BND - size_rows), size_rows, 0
                )
                return tail_rows - jnp.dot(
                    own_below,
                    below.T,
                    precision=highest_precision,
                    preferred_element_type=jnp.float32,
                )

            def empty_term():
                return jnp.zeros((size_rows, BND), jnp.float32)

            difference = lax.cond(holds_tail, tail_term, empty_term)
            leading = difference[:half_rows]
            if level_no == 0:
                received = from_behind(leading, "front", -(front_count // 2))
            else:
                received = from_behind(leading, "leaf", -(1 << level_no - 1))
            outgoing = jnp.where(holds_tail, difference[half_rows:], received)
            gathered = twin_order(collect(outgoing, level_no + 1, False), group_size)
            parent_span = span_leaf * 2
            next_rows = width_all // (front_count * parent_span)
            parent_rank = (leaf_pos & parent_span - 1) * front_count + front_pos
            row_ids = parent_rank * next_rows + jnp.arange(next_rows, dtype=jnp.int32)
            parent_no = leaf_pos >> level_no + 1
            assembled = jnp.zeros((next_rows, width_all), jnp.float32)
            for child_no in range(2):
                index_map = lax.dynamic_slice_in_dim(
                    child_maps, map_base + 2 * parent_no + child_no, 1, 0
                )[0]
                picked = child_rows(gathered[child_no], index_map, row_ids)
                assembled = assembled.at[:, index_map].add(picked)
            assembled = jnp.where(column_ids[None, :] <= row_ids[:, None], assembled, 0.0)
            col_block = coupling_cols[0, 0, list_offset : list_offset + next_rows, :]
            val_block = coupling_vals[0, 0, list_offset : list_offset + next_rows, :]
            local_rows = jnp.arange(next_rows, dtype=jnp.int32)
            assembled = assembled.at[local_rows[:, None], col_block].add(val_block)
            diag_piece = sep_diag[0, 0, list_offset : list_offset + next_rows]
            assembled = assembled + jnp.where(
                column_ids[None, :] == row_ids[:, None], diag_piece[:, None], 0.0
            )
            front_strip = assembled
            list_offset = list_offset + next_rows
            map_base = map_base + group_count // span_leaf
    log_det = 2.0 * lax.psum(log_part, ("leaf", "front"))
    factors = jnp.concatenate(pieces_out, axis=0)[None, None]
    return (factors, log_det)


def solution(mesh):
    placed = (
        P("leaf", "front", None),
        P("leaf", "front", None, None),
        P("leaf", "front", None, None),
        P("leaf", "front", None),
        P(),
    )
    return jax.shard_map(
        body,
        mesh=mesh,
        in_specs=placed,
        out_specs=(P("leaf", "front", None, None), P()),
        check_vma=False,
    )
```

profile of v0, /device:TPU:1, one launch (start us, length us, event | category | flops | bytes accessed | tf_op | source)
XLA Modules:
  0.0 2185.0 jit_solution(17562657626396560996)
XLA Ops:
  9.3 33.1 %all-gather.6.cloned.1.call-done = f32[1024,512]{1,0:T(8,128)} async-done(((f32[128,512]{1,0:T(8,128)}), f32[1024,512]{1,0:T(8,128)}) %all-gather.6.cloned.1.call-update) | async-done | bytes 2097168 | tf_op jit(solution)/shard_map/all_gather | solution.py:43
  152.5 39.3 %custom-call.72 = f32[4,128,128]{1,2,0:T(8,128)S(1)} custom-call(f32[4,128,128]{2,1,0:T(8,128)S(1)} %get-tuple-element.167), custom_call_target="InvertDiagBlocksLowerTriangular" | custom-call | tf_op jit(solution)/shard_map/jit(_solve_triangular)/triangular_solve | solution.py:97
  215.7 23.5 %all-gather.8.cloned.1.call-done = f32[512,512]{1,0:T(8,128)} async-done(((f32[64,512]{1,0:T(8,128)}), f32[512,512]{1,0:T(8,128)}) %all-gather.8.cloned.1.call-update) | async-done | bytes 1048592 | tf_op jit(solution)/shard_map/all_gather | solution.py:45
  243.6 20.4 collective-permute-done.1
  278.8 57.0 %scatter_fusion.6 = f32[65536]{0:T(1024)S(1)} fusion(f32[65536]{0:T(1024)S(1)} %bitcast.497, s32[8192]{0:T(1024)S(1)} %copy-done.34, f32[8192]{0:T(1024)S(1)} %bitcast.526), kind=kCustom, calls=%fused_computation.43 | custom fusion | flops 8192 | bytes 131072
  336.7 26.7 %all-gather.10.cloned.1.call-done = f32[512,512]{1,0:T(8,128)} async-done(((f32[64,512]{1,0:T(8,128)}), f32[512,512]{1,0:T(8,128)}) %all-gather.10.cloned.1.call-update) | async-done | bytes 1048592 | tf_op jit(solution)/shard_map/all_gather | solution.py:43
  365.8 22.4 %collective-permute-done.2 = f32[512,512]{1,0:T(8,128)S(1)} collective-permute-done((f32[512,512]{1,0:T(8,128)}, f32[512,512]{1,0:T(8,128)S(1)}, u32[]{:S(2)}, u32[]{:S(2)}) %collective-permute-start.2) | collective-permute-done | bytes 1048608 | tf_op jit(solution)/shard_map/ppermute | solution.py:20
  500.6 39.9 %custom-call.76 = f32[4,128,128]{1,2,0:T(8,128)} custom-call(f32[4,128,128]{2,1,0:T(8,128)S(1)} %get-tuple-element.168), custom_call_target="InvertDiagBlocksLowerTriangular" | custom-call | tf_op jit(solution)/shard_map/jit(_solve_triangular)/triangular_solve | solution.py:97
  602.7 22.6 %collective-permute-done.5 = f32[512,512]{1,0:T(8,128)} collective-permute-done((f32[512,512]{1,0:T(8,128)}, f32[512,512]{1,0:T(8,128)}, u32[]{:S(2)}, u32[]{:S(2)}) %collective-permute-start.5) | collective-permute-done | bytes 1048608 | tf_op jit(solution)/shard_map/ppermute | solution.py:20
  647.6 28.8 %scatter_fusion.7 = f32[32768]{0:T(1024)S(1)} fusion(f32[32768]{0:T(1024)S(1)} %bitcast.498, s32[4096]{0:T(1024)S(1)} %select_bitcast_fusion.24, f32[4096]{0:T(1024)S(1)} %bitcast.527), kind=kCustom, calls=%fused_computation.44 | custom fusion | flops 4096 | bytes 65536
  708.2 22.3 %collective-permute-done.7 = f32[512,512]{1,0:T(8,128)} collective-permute-done((f32[512,512]{1,0:T(8,128)S(1)}, f32[512,512]{1,0:T(8,128)}, u32[]{:S(2)}, u32[]{:S(2)}) %collective-permute-start.7) | collective-permute-done | bytes 1048608 | tf_op jit(solution)/shard_map/ppermute | solution.py:20
  851.2 39.9 %custom-call.80 = f32[4,128,128]{1,2,0:T(8,128)} custom-call(f32[4,128,128]{2,1,0:T(8,128)S(1)} %get-tuple-element.169), custom_call_target="InvertDiagBlocksLowerTriangular" | custom-call | tf_op jit(solution)/shard_map/jit(_solve_triangular)/triangular_solve | solution.py:97
  961.3 21.7 collective-permute-done.11
  1059.3 21.6 collective-permute-done.14
  1198.1 39.9 %custom-call.84 = f32[4,128,128]{1,2,0:T(8,128)} custom-call(f32[4,128,128]{2,1,0:T(8,128)S(1)} %get-tuple-element.170), custom_call_target="InvertDiagBlocksLowerTriangular" | custom-call | tf_op jit(solution)/shard_map/jit(_solve_triangular)/triangular_solve | solution.py:97
  1314.1 45.0 %collective-permute-done.19 = f32[512,512]{1,0:T(8,128)} collective-permute-done((f32[512,512]{1,0:T(8,128)}, f32[512,512]{1,0:T(8,128)}, u32[]{:S(2)}, u32[]{:S(2)}) %collective-permute-start.19) | collective-permute-done | bytes 1048608 | tf_op jit(solution)/shard_map/ppermute | solution.py:20
  1431.5 45.2 %collective-permute-done.23 = f32[512,512]{1,0:T(8,128)} collective-permute-done((f32[512,512]{1,0:T(8,128)S(1)}, f32[512,512]{1,0:T(8,128)}, u32[]{:S(2)}, u32[]{:S(2)}) %collective-permute-start.23) | collective-permute-done | bytes 1048608 | tf_op jit(solution)/shard_map/ppermute | solution.py:20
  1594.0 39.9 %custom-call.88 = f32[4,128,128]{1,2,0:T(8,128)} custom-call(f32[4,128,128]{2,1,0:T(8,128)S(1)} %get-tuple-element.171), custom_call_target="InvertDiagBlocksLowerTriangular" | custom-call | tf_op jit(solution)/shard_map/jit(_solve_triangular)/triangular_solve | solution.py:97
  1695.8 22.6 %collective-permute-done.28 = f32[256,512]{1,0:T(8,128)} collective-permute-done((f32[256,512]{1,0:T(8,128)S(1)}, f32[256,512]{1,0:T(8,128)}, u32[]{:S(2)}, u32[]{:S(2)}) %collective-permute-start.28) | collective-permute-done | bytes 524320 | tf_op jit(solution)/shard_map/ppermute | solution.py:20
  1722.7 47.7 %collective-permute-done.29 = f32[512,512]{1,0:T(8,128)} collective-permute-done((f32[512,512]{1,0:T(8,128)}, f32[512,512]{1,0:T(8,128)}, u32[]{:S(2)}, u32[]{:S(2)}) %collective-permute-start.29) | collective-permute-done | bytes 1048608 | tf_op jit(solution)/shard_map/ppermute | solution.py:20
  1801.1 24.8 %scatter_fusion.5 = f32[4,1024]{1,0:T(4,128)S(1)} fusion(f32[4,1024]{1,0:T(4,128)S(1)} %add.625, s32[512]{0:T(512)S(1)} %fusion.262, f32[512]{0:T(512)S(1)} %bitcast.530), kind=kCustom, calls=%fused_computation.42 | custom fusion | flops 512 | bytes 10240 | tf_op jit(solution)/shard_map/scatter-add | solution.py:148
  1913.9 20.8 collective-permute-done.34
  2040.2 39.3 %custom-call.92 = f32[4,128,128]{1,2,0:T(8,128)S(1)} custom-call(f32[4,128,128]{2,1,0:T(8,128)S(1)} %get-tuple-element.172), custom_call_target="InvertDiagBlocksLowerTriangular" | custom-call | tf_op jit(solution)/shard_map/jit(_solve_triangular)/triangular_solve | solution.py:97
  2095.1 76.0 %psum.7 = f32[]{:T(128)} all-reduce(f32[]{:T(128)S(6)} %add.634), channel_id=1, replica_groups=mesh['leaf'=32,'front'=8] {'leaf','front'}, use_global_device_ids=true, to_apply=%region_59.72 | all-reduce | flops 1 | bytes 8 | tf_op jit(solution)/shard_map/psum | solution.py:156
  (831 shorter events, 1395.4 us)
Async XLA Ops:
  7.2 35.2 %all-gather.6.cloned.1.call-start = ((), (), s32[]{:S(2)}) async-start(), calls=%async_computation | async-start | bytes 2359296 | tf_op jit(solution)/shard_map/all_gather | solution.py:43
  9.2 230.0 %all-gather.8.cloned.1.call-start = ((), (), s32[]{:S(2)}) async-start(), calls=%async_computation.1 | async-start | bytes 1179648 | tf_op jit(solution)/shard_map/all_gather | solution.py:45
  204.3 8.8 collective-permute-start
  213.7 149.7 %all-gather.10.cloned.1.call-start = ((), (), s32[]{:S(2)}) async-start(), calls=%async_computation.2 | async-start | bytes 1179648 | tf_op jit(solution)/shard_map/all_gather | solution.py:43
  239.2 24.7 %collective-permute-start.1 = (f32[512,512]{1,0:T(8,128)}, f32[512,512]{1,0:T(8,128)S(1)}, u32[]{:S(2)}, u32[]{:S(2)}) collective-permute-start(f32[512,512]{1,0:T(8,128)} %all-gather.8.cloned.1.call-done), channel_id=1, source_target_pairs={{0,8},{8,0},{16,24},{24,16},{32,40},{40,32},{48,56},{56,48},{64,72... | collective-permute-start | bytes 3145736 | tf_op jit(solution)/shard_map/ppermute | solution.py:20
  363.4 24.7 %collective-permute-start.2 = (f32[512,512]{1,0:T(8,128)}, f32[512,512]{1,0:T(8,128)S(1)}, u32[]{:S(2)}, u32[]{:S(2)}) collective-permute-start(f32[512,512]{1,0:T(8,128)} %all-gather.10.cloned.1.call-done), channel_id=1, source_target_pairs={{0,8},{8,0},{16,24},{24,16},{32,40},{40,32},{48,56},{56,48},{64,72... | collective-permute-start | bytes 3145736 | tf_op jit(solution)/shard_map/ppermute | solution.py:20
  582.4 14.0 collective-permute-start.4
  597.6 27.7 %collective-permute-start.5 = (f32[512,512]{1,0:T(8,128)}, f32[512,512]{1,0:T(8,128)}, u32[]{:S(2)}, u32[]{:S(2)}) collective-permute-start(f32[512,512]{1,0:T(8,128)} %pad_maximum_fusion.7), channel_id=1, source_target_pairs={{0,16},{16,0},{8,24},{24,8},{32,48},{48,32},{40,56},{56,40},{64,80... | collective-permute-start | bytes 3145736 | tf_op jit(solution)/shard_map/ppermute | solution.py:20
  690.8 13.4 collective-permute-start.6
  705.2 25.3 %collective-permute-start.7 = (f32[512,512]{1,0:T(8,128)S(1)}, f32[512,512]{1,0:T(8,128)}, u32[]{:S(2)}, u32[]{:S(2)}) collective-permute-start(f32[512,512]{1,0:T(8,128)S(1)} %pad_maximum_fusion.8), channel_id=1, source_target_pairs={{0,16},{16,0},{8,24},{24,8},{32,48},{48,32},{40,56},{56,40},{64,80... | collective-permute-start | bytes 3145736 | tf_op jit(solution)/shard_map/ppermute | solution.py:20
  942.7 15.5 collective-permute-start.10
  959.4 23.6 %collective-permute-start.11 = (f32[512,512]{1,0:T(8,128)}, f32[512,512]{1,0:T(8,128)}, u32[]{:S(2)}, u32[]{:S(2)}) collective-permute-start(f32[512,512]{1,0:T(8,128)} %pad_maximum_fusion.10), channel_id=1, source_target_pairs={{0,32},{32,0},{8,40},{40,8},{16,48},{48,16},{24,56},{56,24},{64,96... | collective-permute-start | bytes 3145736 | tf_op jit(solution)/shard_map/ppermute | solution.py:20
  1042.9 14.0 collective-permute-start.13
  1058.1 22.9 %collective-permute-start.14 = (f32[512,512]{1,0:T(8,128)S(1)}, f32[512,512]{1,0:T(8,128)}, u32[]{:S(2)}, u32[]{:S(2)}) collective-permute-start(f32[512,512]{1,0:T(8,128)S(1)} %pad_maximum_fusion.11), channel_id=1, source_target_pairs={{0,32},{32,0},{8,40},{40,8},{16,48},{48,16},{24,56},{56,24},{64,96... | collective-permute-start | bytes 3145736 | tf_op jit(solution)/shard_map/ppermute | solution.py:20
  1285.6 8.4 collective-permute-start.17
  1294.1 12.2 collective-permute-start.18
  1307.4 51.7 %collective-permute-start.19 = (f32[512,512]{1,0:T(8,128)}, f32[512,512]{1,0:T(8,128)}, u32[]{:S(2)}, u32[]{:S(2)}) collective-permute-start(f32[512,512]{1,0:T(8,128)} %pad_maximum_fusion.13), channel_id=1, source_target_pairs={{0,64},{64,0},{8,72},{72,8},{16,80},{80,16},{24,88},{88,24},{32,96... | collective-permute-start | bytes 3145736 | tf_op jit(solution)/shard_map/ppermute | solution.py:20
  1407.9 8.4 collective-permute-start.21
  1416.4 11.6 collective-permute-start.22
  1429.1 47.6 %collective-permute-start.23 = (f32[512,512]{1,0:T(8,128)S(1)}, f32[512,512]{1,0:T(8,128)}, u32[]{:S(2)}, u32[]{:S(2)}) collective-permute-start(f32[512,512]{1,0:T(8,128)S(1)} %pad_maximum_fusion.14), channel_id=1, source_target_pairs={{0,64},{64,0},{8,72},{72,8},{16,80},{80,16},{24,88},{88,24},{32,96... | collective-permute-start | bytes 3145736 | tf_op jit(solution)/shard_map/ppermute | solution.py:20
  1691.6 26.7 %collective-permute-start.28 = (f32[256,512]{1,0:T(8,128)S(1)}, f32[256,512]{1,0:T(8,128)}, u32[]{:S(2)}, u32[]{:S(2)}) collective-permute-start(f32[256,512]{1,0:T(8,128)S(1)} %pad_maximum_fusion.22), channel_id=1, source_target_pairs={{0,64},{64,0},{8,72},{72,8},{16,80},{80,16},{24,88},{88,24},{32,96... | collective-permute-start | bytes 1572872 | tf_op jit(solution)/shard_map/ppermute | solution.py:20
  1720.6 49.7 %collective-permute-start.29 = (f32[512,512]{1,0:T(8,128)}, f32[512,512]{1,0:T(8,128)}, u32[]{:S(2)}, u32[]{:S(2)}) collective-permute-start(f32[512,512]{1,0:T(8,128)} %pad_maximum_fusion.16), channel_id=1, source_target_pairs={{0,128},{128,0},{8,136},{136,8},{16,144},{144,16},{24,152},{152,24... | collective-permute-start | bytes 3145736 | tf_op jit(solution)/shard_map/ppermute | solution.py:20
  1855.2 25.5 %collective-permute-start.33 = (f32[256,512]{1,0:T(8,128)S(1)}, f32[256,512]{1,0:T(8,128)}, u32[]{:S(2)}, u32[]{:S(2)}) collective-permute-start(f32[256,512]{1,0:T(8,128)S(1)} %pad_maximum_fusion.23), channel_id=1, source_target_pairs={{0,64},{64,0},{8,72},{72,8},{16,80},{80,16},{24,88},{88,24},{32,96... | collective-permute-start | bytes 1572872 | tf_op jit(solution)/shard_map/ppermute | solution.py:20
  1883.1 51.6 %collective-permute-start.34 = (f32[512,512]{1,0:T(8,128)}, f32[512,512]{1,0:T(8,128)}, u32[]{:S(2)}, u32[]{:S(2)}) collective-permute-start(f32[512,512]{1,0:T(8,128)} %pad_maximum_fusion.17), channel_id=1, source_target_pairs={{0,128},{128,0},{8,136},{136,8},{16,144},{144,16},{24,152},{152,24... | collective-permute-start | bytes 3145736 | tf_op jit(solution)/shard_map/ppermute | solution.py:20
  (90 other events, 1269.6 us)
Sparse Core Ops, SparseCore 0:
  10.4 31.8 all-gather.5
  213.9 25.3 all-gather.7
  336.8 26.5 all-gather.9
where the time goes:
time: 2200 us; the launch traced here: 2180 us
  other arithmetic  971 us (44%)
  waiting for transfers between devices  565 us (26%)
  local copies, waits for them, and re-layouts  249 us (11%)
  blocking collectives  195 us (9%)
  matrix products  98.3 us (4%)
  starting transfers between devices  68.1 us (3%)
  between operations  37.8 us (2%)
    another operation x89, other arithmetic, body(): chol_head = jnp.linalg.cholesky(head_block)  479 us
    ppermute x30, waiting for transfers between devices, swapped(): return lax.ppermute(block, axis, route)  454 us
    another operation x18, other arithmetic, body(): jax.scipy.linalg.solve_triangular(chol_head, panel_cols[SEP:].T, lower=True)  258 us
    all_gather x8, blocking collectives, collect(): gathered = lax.all_gather(strip_piece, 'front', axis=0, tiled=True)  119 us
    unnamed x22, other arithmetic  113 us
    another operation x97, local copies, waits for them, and re-layouts, body(): jax.scipy.linalg.solve_triangular(chol_head, panel_cols[SEP:].T, lower=True)  89.5 us
    all_gather x3, waiting for transfers between devices, collect(): gathered = lax.all_gather(strip_piece, 'front', axis=0, tiled=True)  83.3 us
    psum x1, blocking collectives, body(): log_det = 2.0 * lax.psum(log_part, ('leaf', 'front'))  76 us
  transfers between devices with their start and end apart: 38, of which 38 were waited for; matrix products, arithmetic and copies ran while one was open for 2% of the time, Pallas kernels for 0%

commit v1 on v0

v1 whole, which is shorter than its diff:
```python
import functools

import jax
import jax.numpy as jnp
from jax import lax
from jax.experimental import pallas as pl
from jax.experimental.pallas import tpu as pltpu
from jax.sharding import PartitionSpec as P

SEP = 512
BND = 512
WIDE = SEP + BND
NB = 128
F32 = jnp.float32
BF16 = jnp.bfloat16
MESH = pl.DeviceIdType.MESH
VMEM_SPEC = pl.BlockSpec(memory_space=pltpu.VMEM)
SMEM_SPEC = pl.BlockSpec(memory_space=pltpu.SMEM)
ANY_SPEC = pl.BlockSpec(memory_space=pl.ANY)
VMEM_LIMIT = 48 * 2**20


def split2(a):
    hi = a.astype(BF16)
    lo = (a - hi.astype(F32)).astype(BF16)
    return hi, lo


def dg(a, b, ca, cb):
    return lax.dot_general(a, b, (((ca,), (cb,)), ((), ())), preferred_element_type=F32)


def dot3(a, b):
    ah, al = split2(a)
    bh, bl = split2(b)
    return dg(ah, bh, 1, 0) + (dg(ah, bl, 1, 0) + dg(al, bh, 1, 0))


def row_of(x, j):
    return jnp.broadcast_to(x[j : j + 1, :], (8, NB))


def col_of(x, k):
    return jnp.broadcast_to(x[:, k : k + 1], (8, NB))


def diag_factor(dref, nref):
    sub = lax.broadcasted_iota(jnp.int32, (8, NB), 0)
    lane = lax.broadcasted_iota(jnp.int32, (8, NB), 1)
    zero = jnp.zeros((8, NB), F32)
    D = [dref[8 * v : 8 * v + 8, :] for v in range(16)]
    N = [jnp.where(lane == sub + 8 * v, 1.0, 0.0) for v in range(16)]
    for b in range(16):
        cols = [col_of(D[b], 8 * b + k) for k in range(8)]
        a = {(i, k): row_of(cols[k], i) for k in range(8) for i in range(k, 8)}
        drow = [row_of(D[b], j) for j in range(8)]
        nrow = [row_of(N[b], j) for j in range(8)]
        r, l, u, n = {}, {}, [], []
        for j in range(8):
            r[j] = lax.rsqrt(a[j, j])
            for i in range(j + 1, 8):
                l[i, j] = a[i, j] * r[j]
            for k in range(j + 1, 8):
                for i in range(k, 8):
                    a[i, k] = a[i, k] - l[i, j] * l[k, j]
            u.append(drow[j] * r[j])
            n.append(nrow[j] * r[j])
            for i in range(j + 1, 8):
                drow[i] = drow[i] - l[i, j] * u[j]
                nrow[i] = nrow[i] - l[i, j] * n[j]
        for v in range(b + 1, 16):
            c = [col_of(D[v], 8 * b + k) for k in range(8)]
            dv, nv = D[v], N[v]
            for j in range(8):
                lj = c[j] * r[j]
                for k in range(j + 1, 8):
                    c[k] = c[k] - lj * l[k, j]
                dv = dv - lj * u[j]
                nv = nv - lj * n[j]
            D[v], N[v] = dv, nv
        db, nb = u[0], n[0]
        for j in range(1, 8):
            db = jnp.where(sub == j, u[j], db)
            nb = jnp.where(sub == j, n[j], nb)
        D[b] = jnp.where(lane >= 8 * b + sub, db, zero)
        N[b] = nb
        dref[8 * b : 8 * b + 8, :] = D[b]
        nref[8 * b : 8 * b + 8, :] = N[b]


def fac_kernel(with_update, size_rows, *refs):
    if with_update:
        pos_ref, t_ref, tail_ref, log_in, piece_ref, log_ref, upd_ref, u_ref, d_ref, n_ref, p_ref = refs
    else:
        pos_ref, t_ref, log_in, piece_ref, log_ref, u_ref, d_ref, n_ref, p_ref = refs
    u_ref[...] = t_ref[...]
    log_ref[...] = log_in[...]
    rows = lax.broadcasted_iota(jnp.int32, (NB, NB), 0)
    cols = lax.broadcasted_iota(jnp.int32, (NB, NB), 1)
    wide = lax.broadcasted_iota(jnp.int32, (NB, WIDE), 1)

    @pl.loop(0, SEP // NB)
    def block(blk):
        o = pl.multiple_of(blk * NB, NB)
        d_ref[...] = u_ref[pl.ds(o, NB), pl.ds(o, NB)]
        diag_factor(d_ref, n_ref)
        d = d_ref[...]
        logs = jnp.where(rows == cols, jnp.log(d), 0.0)
        log_ref[...] += 2.0 * jnp.sum(logs.reshape(16, 8, NB), axis=0)
        strip = dot3(n_ref[...], u_ref[pl.ds(o, NB), :])
        strip = jnp.where(wide >= o + NB, strip, 0.0)
        u_ref[pl.ds(o, NB), :] = strip
        u_ref[pl.ds(o, NB), pl.ds(o, NB)] = d
        sh, sl = split2(strip)

        @pl.loop(blk + 1, SEP // NB)
        def trail(jb):
            q = pl.multiple_of(jb * NB, NB)
            lh, ll = split2(u_ref[pl.ds(o, NB), pl.ds(q, NB)].T)
            u_ref[pl.ds(q, NB), :] -= dg(lh, sh, 1, 0) + (dg(lh, sl, 1, 0) + dg(ll, sh, 1, 0))

    if with_update:
        below = u_ref[:, SEP:]
        bh, bl = split2(below)
        th, tl = split2(below.T)
        upd_ref[...] = tail_ref[...] - (dg(th, bh, 1, 0) + (dg(th, bl, 1, 0) + dg(tl, bh, 1, 0)))
    start = pos_ref[0]
    base = pl.multiple_of(start // NB * NB, NB)
    p_ref[...] = u_ref[:, pl.ds(base, NB)].T
    if size_rows % 8 == 0:
        piece_ref[...] = p_ref[pl.ds(pl.multiple_of(start - base, 8), size_rows), :]
    else:
        part = start % 8
        block8 = p_ref[pl.ds(pl.multiple_of(start - base - part, 8), 8), :]
        picked = block8[:size_rows]
        for first in range(size_rows, 8, size_rows):
            picked = jnp.where(part == first, block8[first : first + size_rows], picked)
        piece_ref[...] = picked


def factor(pos, t, tail, log_acc, size_rows):
    with_update = tail is not None
    outs = [jax.ShapeDtypeStruct((size_rows, SEP), F32), jax.ShapeDtypeStruct((8, NB), F32)]
    if with_update:
        outs.append(jax.ShapeDtypeStruct((BND, BND), F32))
    args = (pos, t, tail, log_acc) if with_update else (pos, t, log_acc)
    return pl.pallas_call(
        functools.partial(fac_kernel, with_update, size_rows),
        out_shape=outs,
        in_specs=[SMEM_SPEC] + [VMEM_SPEC] * (len(args) - 1),
        out_specs=[VMEM_SPEC] * len(outs),
        scratch_shapes=[
            pltpu.VMEM((SEP, WIDE), F32),
            pltpu.VMEM((NB, NB), F32),
            pltpu.VMEM((NB, NB), F32),
            pltpu.VMEM((NB, SEP), F32),
        ],
        compiler_params=pltpu.CompilerParams(vmem_limit_bytes=VMEM_LIMIT),
    )(*args)


def mirrored(square):
    rows = lax.broadcasted_iota(jnp.int32, square.shape, 0)
    cols = lax.broadcasted_iota(jnp.int32, square.shape, 1)
    return jnp.where(rows >= cols, square, square.T)


def asm_kernel(child_count, *refs):
    low_ref = refs[0]
    children = refs[1 : 1 + 2 * child_count]
    t_ref, tail_ref = refs[1 + 2 * child_count :]
    t_sum, tail_sum = None, None
    for child in range(child_count):
        upd_ref, map_ref = children[2 * child : 2 * child + 2]
        ids = lax.broadcasted_iota(jnp.int32, (WIDE, BND), 0)
        pick = jnp.where(ids == map_ref[...], 1.0, 0.0).astype(BF16)
        uh, ul = split2(upd_ref[...])
        xh = dg(pick, uh, 1, 0).astype(BF16)
        xl = dg(pick, ul, 1, 0).astype(BF16)
        t_part = dg(xh[:SEP], pick, 1, 1) + dg(xl[:SEP], pick, 1, 1)
        tail_part = dg(xh[SEP:], pick[SEP:], 1, 1) + dg(xl[SEP:], pick[SEP:], 1, 1)
        if child == 0:
            t_ref[...] = t_part
            tail_ref[...] = tail_part
        else:
            t_ref[...] += t_part
            tail_ref[...] += tail_part
    head = mirrored(low_ref[:SEP, :SEP])
    side = low_ref[SEP:, :SEP].T
    tail = mirrored(low_ref[SEP:, SEP:])
    if child_count:
        t_ref[:, :SEP] += head
        t_ref[:, SEP:] += side
        tail_ref[...] += tail
    else:
        t_ref[:, :SEP] = head
        t_ref[:, SEP:] = side
        tail_ref[...] = tail


def assemble(low, children):
    flat = [part for child in children for part in child]
    return pl.pallas_call(
        functools.partial(asm_kernel, len(children)),
        out_shape=[jax.ShapeDtypeStruct((SEP, WIDE), F32), jax.ShapeDtypeStruct((BND, BND), F32)],
        in_specs=[VMEM_SPEC] * (1 + len(flat)),
        out_specs=[VMEM_SPEC] * 2,
        compiler_params=pltpu.CompilerParams(vmem_limit_bytes=VMEM_LIMIT),
    )(low, *flat)


def couple_kernel(cols_ref, vals_ref, diag_ref, ids_ref, out_ref):
    lane = lax.broadcasted_iota(jnp.int32, (8, NB), 1)

    @pl.loop(0, cols_ref.shape[0] // 8)
    def group(g):
        at = pl.ds(pl.multiple_of(g * 8, 8), 8)
        cols, vals = cols_ref[at, :], vals_ref[at, :]
        row_id = jnp.broadcast_to(ids_ref[at, :], (8, NB))
        diag = jnp.broadcast_to(diag_ref[at, :], (8, NB))
        sums = [jnp.where(row_id == lane + NB * c, diag, 0.0) for c in range(8)]
        for k in range(NB):
            col, val = col_of(cols, k), col_of(vals, k)
            for c in range(8):
                sums[c] = sums[c] + jnp.where(col == lane + NB * c, val, 0.0)
        for c in range(8):
            out_ref[at, NB * c : NB * c + NB] = sums[c]


def couple(cols, vals, diag, ids):
    return pl.pallas_call(
        couple_kernel,
        out_shape=jax.ShapeDtypeStruct((cols.shape[0], WIDE), F32),
        in_specs=[VMEM_SPEC] * 4,
        out_specs=VMEM_SPEC,
        compiler_params=pltpu.CompilerParams(vmem_limit_bytes=VMEM_LIMIT),
    )(cols, vals, diag, ids)


def gather_kernel(count, strip_ref, out_ref, own_sem, send_sem, recv_sem, fsend_sem, frecv_sem):
    me = lax.axis_index("front")
    rows = strip_ref.shape[0]
    chips = count // 2
    chip, core = me // 2, lax.rem(me, 2)
    twin = chip * 2 + 1 - core
    barrier = pltpu.get_barrier_semaphore()
    peers = [lax.rem(chip + d, chips) * 2 + core for d in range(1, chips)]
    for peer in peers + [twin]:
        pl.semaphore_signal(barrier, inc=1, device_id={"front": peer}, device_id_type=MESH)
    pl.semaphore_wait(barrier, chips)

    def at(index):
        return out_ref.at[pl.ds(pl.multiple_of(index * rows, rows), rows), :]

    own = pltpu.make_async_copy(strip_ref, at(me), own_sem)
    own.start()
    first = []
    for d in range(1, chips):
        peer = peers[d - 1]
        copy = pltpu.make_async_remote_copy(
            src_ref=strip_ref, dst_ref=at(me), send_sem=send_sem.at[d - 1], recv_sem=recv_sem.at[d - 1],
            device_id={"front": peer}, device_id_type=MESH,
        )
        copy.start()
        first.append(copy)
    second = []
    for d in range(chips):
        if d == 0:
            src, index = strip_ref, me
        else:
            index = lax.rem(chip - d + chips, chips) * 2 + core
            src = at(index)
            first[d - 1].wait_recv()
        copy = pltpu.make_async_remote_copy(
            src_ref=src, dst_ref=at(index), send_sem=fsend_sem.at[d], recv_sem=frecv_sem.at[d],
            device_id={"front": twin}, device_id_type=MESH,
        )
        copy.start()
        second.append(copy)
    own.wait()
    for copy in second:
        copy.wait_recv()
    for copy in first + second:
        copy.wait_send()


def gather_front(strip, count, cid):
    chips = count // 2
    return pl.pallas_call(
        functools.partial(gather_kernel, count),
        out_shape=jax.ShapeDtypeStruct((count * strip.shape[0], strip.shape[1]), F32),
        in_specs=[VMEM_SPEC],
        out_specs=VMEM_SPEC,
        scratch_shapes=[
            pltpu.SemaphoreType.DMA,
            pltpu.SemaphoreType.DMA((chips,)),
            pltpu.SemaphoreType.DMA((chips,)),
            pltpu.SemaphoreType.DMA((chips,)),
            pltpu.SemaphoreType.DMA((chips,)),
        ],
        compiler_params=pltpu.CompilerParams(
            collective_id=cid, has_side_effects=True, vmem_limit_bytes=VMEM_LIMIT
        ),
    )(strip)


def swap_kernel(count, bit, upd_ref, log_ref, out_ref, log_out, sems, first_sem, send_sem, recv_sem, fsend_sem, frecv_sem):
    leaf = lax.axis_index("leaf")
    me = lax.axis_index("front")
    side = lax.rem(leaf // (1 << bit), 2)
    other = leaf + (1 - 2 * side) * (1 << bit)
    rows = upd_ref.shape[0] // count
    chips = count // 2
    chip, core = me // 2, lax.rem(me, 2)
    twin = chip * 2 + 1 - core
    barrier = pltpu.get_barrier_semaphore()
    peers = [lax.rem(chip + d, chips) * 2 + core for d in range(1, chips)]
    pl.semaphore_signal(barrier, inc=1, device_id={"leaf": other}, device_id_type=MESH)
    for peer in peers + [twin]:
        pl.semaphore_signal(barrier, inc=1, device_id={"front": peer}, device_id_type=MESH)
    pl.semaphore_wait(barrier, chips + 1)

    def at(ref, index):
        return ref.at[pl.ds(pl.multiple_of(index * rows, rows), rows), :]

    cross = pltpu.make_async_remote_copy(
        src_ref=at(upd_ref, me), dst_ref=at(out_ref, me), send_sem=first_sem.at[0], recv_sem=first_sem.at[1],
        device_id={"leaf": other}, device_id_type=MESH,
    )
    cross.start()
    logs = pltpu.make_async_remote_copy(
        src_ref=log_ref, dst_ref=log_out, send_sem=sems.at[0], recv_sem=sems.at[1],
        device_id={"leaf": other}, device_id_type=MESH,
    )
    logs.start()
    cross.wait_recv()
    first = []
    for d in range(1, chips):
        copy = pltpu.make_async_remote_copy(
            src_ref=at(out_ref, me), dst_ref=at(out_ref, me), send_sem=send_sem.at[d - 1], recv_sem=recv_sem.at[d - 1],
            device_id={"front": peers[d - 1]}, device_id_type=MESH,
        )
        copy.start()
        first.append(copy)
    second = []
    for d in range(chips):
        index = lax.rem(chip - d + chips, chips) * 2 + core
        if d:
            first[d - 1].wait_recv()
        copy = pltpu.make_async_remote_copy(
            src_ref=at(out_ref, index), dst_ref=at(out_ref, index), send_sem=fsend_sem.at[d], recv_sem=frecv_sem.at[d],
            device_id={"front": twin}, device_id_type=MESH,
        )
        copy.start()
        second.append(copy)
    logs.wait_recv()
    for copy in second:
        copy.wait_recv()
    for copy in [cross, logs] + first + second:
        copy.wait_send()


def swap_siblings(upd, log_acc, count, bit, cid):
    chips = count // 2
    return pl.pallas_call(
        functools.partial(swap_kernel, count, bit),
        out_shape=[jax.ShapeDtypeStruct(upd.shape, F32), jax.ShapeDtypeStruct(log_acc.shape, F32)],
        in_specs=[VMEM_SPEC] * 2,
        out_specs=[VMEM_SPEC] * 2,
        scratch_shapes=[
            pltpu.SemaphoreType.DMA((2,)),
            pltpu.SemaphoreType.DMA((2,)),
            pltpu.SemaphoreType.DMA((chips,)),
            pltpu.SemaphoreType.DMA((chips,)),
            pltpu.SemaphoreType.DMA((chips,)),
            pltpu.SemaphoreType.DMA((chips,)),
        ],
        compiler_params=pltpu.CompilerParams(
            collective_id=cid, has_side_effects=True, vmem_limit_bytes=VMEM_LIMIT
        ),
    )(upd, log_acc)


def body(leaf_fronts, coupling_cols, coupling_vals, sep_diag, child_maps):
    group_count = lax.axis_size("leaf")
    front_count = lax.axis_size("front")
    level_total = group_count.bit_length()
    leaf_pos = lax.axis_index("leaf")
    front_pos = lax.axis_index("front")
    pieces_out = []

    id_list = []
    for level_no in range(1, level_total):
        size_rows = WIDE // (front_count << level_no)
        rank = (leaf_pos & (1 << level_no) - 1) * front_count + front_pos
        id_list.append(rank * size_rows + jnp.arange(size_rows, dtype=jnp.int32))
    ids = jnp.concatenate(id_list)
    row_total = ids.shape[0]
    pad = -row_total % 8
    cols = jnp.pad(coupling_cols[0, 0], ((0, pad), (0, 0)))
    vals = jnp.pad(coupling_vals[0, 0], ((0, pad), (0, 0)))
    diag = jnp.pad(sep_diag[0, 0], (0, pad))[:, None]
    ids = jnp.pad(ids, (0, pad))[:, None]
    dense = couple(cols, vals, diag, ids)
    lows = []
    offset = 0
    for level_no in range(1, level_total):
        size_rows = WIDE // (front_count << level_no)
        span = 1 << level_no
        strip = dense[offset : offset + size_rows]
        groups = [
            [(g * span + a) * front_count + f for a in range(span) for f in range(front_count)]
            for g in range(group_count // span)
        ]
        lows.append(
            lax.all_gather(strip, ("leaf", "front"), axis=0, tiled=True, axis_index_groups=groups)
            if len(groups) > 1
            else lax.all_gather(strip, ("leaf", "front"), axis=0, tiled=True)
        )
        offset += size_rows

    low = gather_front(leaf_fronts[0], front_count, 0)
    log_acc = jnp.zeros((8, NB), F32)
    t, tail = assemble(low, [])
    map_base = 0
    for level_no in range(level_total):
        span = 1 << level_no
        size_rows = WIDE // (front_count * span)
        rank = (leaf_pos & span - 1) * front_count + front_pos
        pos = jnp.full((1,), rank * size_rows, jnp.int32)
        if level_no + 1 == level_total:
            piece, log_acc = factor(pos, t, None, log_acc, size_rows)
            pieces_out.append(piece)
            break
        piece, log_acc, upd = factor(pos, t, tail, log_acc, size_rows)
        pieces_out.append(piece)
        sib, sib_log = swap_siblings(upd, log_acc, front_count, level_no, 1 + level_no)
        log_acc = log_acc + sib_log
        own_no = leaf_pos >> level_no
        own_map = lax.dynamic_slice_in_dim(child_maps, map_base + own_no, 1, 0)
        sib_map = lax.dynamic_slice_in_dim(child_maps, map_base + (own_no ^ 1), 1, 0)
        t, tail = assemble(lows[level_no], [(upd, own_map), (sib, sib_map)])
        map_base += group_count // span
    log_det = jnp.sum(log_acc)
    factors = jnp.concatenate(pieces_out, axis=0)[None, None]
    return (factors, log_det)


def solution(mesh):
    placed = (
        P("leaf", "front", None),
        P("leaf", "front", None, None),
        P("leaf", "front", None, None),
        P("leaf", "front", None),
        P(),
    )
    return jax.shard_map(
        body,
        mesh=mesh,
        in_specs=placed,
        out_specs=(P("leaf", "front", None, None), P()),
        check_vma=False,
    )
```

time: 2200 us -> 620 us (0.28)
  other arithmetic: 971 us -> 0.64 us
  Pallas kernels: 0 us -> 330 us
  waiting for transfers between devices: 565 us -> 247 us
  local copies, waits for them, and re-layouts: 249 us -> 18.9 us
  blocking collectives: 195 us -> 0 us
  matrix products: 98.3 us -> 0 us
  starting transfers between devices: 68.1 us -> 0.21 us
  between operations: 37.8 us -> 14.6 us
    another operation x112 -> x0, other arithmetic: 738 us -> none  [the longest x89 479 us: body(): chol_head = jnp.linalg.cholesky(head_block)]
    ppermute x35 -> x0, waiting for transfers between devices: 482 us -> none  [the longest x30 454 us: swapped(): return lax.ppermute(block, axis, route)]
    pallas_call x0 -> x19, Pallas kernels: none -> 330 us  [the longest x6 136 us: factor(): pl.pallas_call(functools.partial(fac_kernel, with_update, size_rows), out...]
    all_gather x3 -> x5, waiting for transfers between devices: 83.3 us -> 247 us  [the longest x4 178 us: body(): lax.all_gather(strip, ('leaf', 'front'), axis=0, tiled=True, axis_index_g...]
    all_gather x8 -> x0, blocking collectives: 119 us -> none  [collect(): gathered = lax.all_gather(strip_piece, 'front', axis=0, tiled=True)]
    unnamed x22 -> x0, other arithmetic: 113 us -> none
    another operation x78 -> x0, matrix products: 98.3 us -> none  [the longest x42 69.1 us: body(): jax.scipy.linalg.solve_triangular(chol_head, panel_cols[SEP:].T, lower=True)]
    another operation x130 -> x0, local copies, waits for them, and re-layouts: 91.7 us -> none  [the longest x97 89.5 us: body(): jax.scipy.linalg.solve_triangular(chol_head, panel_cols[SEP:].T, lower=True)]
  transfers between devices with their start and end apart: 38 -> 5, of which waited for: 38 -> 3; matrix products, arithmetic and copies ran while one was open for 2% -> 1% of each run, Pallas kernels for 0% -> 48%
where the time goes in v1:
time: 620 us; the launch traced here: 612 us
  Pallas kernels  330 us (53%)
  waiting for transfers between devices  247 us (40%)
  local copies, waits for them, and re-layouts  18.9 us (3%)
  between operations  14.6 us (2%)
    all_gather x4, waiting for transfers between devices, body(): lax.all_gather(strip, ('leaf', 'front'), axis=0, tiled=True, axis_index_g...  178 us
    pallas_call x6, Pallas kernels, factor(): pl.pallas_call(functools.partial(fac_kernel, with_update, size_rows), out...  136 us
    pallas_call x5, Pallas kernels, swap_siblings(): pl.pallas_call(functools.partial(swap_kernel, count, bit), out_shape=[jax...  96.7 us
    all_gather x1, waiting for transfers between devices, body(): lax.all_gather(strip, ('leaf', 'front'), axis=0, tiled=True)  68.4 us
    pallas_call x1, Pallas kernels, gather_front(): pl.pallas_call(functools.partial(gather_kernel, count), out_shape=jax.Sha...  45.9 us
    pallas_call x6, Pallas kernels, assemble(): pl.pallas_call(functools.partial(asm_kernel, len(children)), out_shape=[j...  43.4 us
    unnamed x18, local copies, waits for them, and re-layouts  14.3 us
  transfers between devices with their start and end apart: 5, of which 3 were waited for; matrix products, arithmetic and copies ran while one was open for 1% of the time, Pallas kernels for 48%

profile of v1, /device:TPU:1, one launch (start us, length us, event | category | flops | bytes accessed | tf_op | source)
XLA Modules:
  0.0 611.6 jit_solution(2419181041919334830)
XLA Ops:
  10.0 8.3 %shard_map.71 = f32[128,1024]{1,0:T(8,128)S(1)} custom-call(s32[128,128]{1,0:T(8,128)S(1)} %pad.16.cols_ref, f32[128,128]{1,0:T(8,128)S(1)} %pad.17.vals_ref, f32[128,1]{1,0:T(8,128)S(1)} %copy.10.diag_ref, s32[128,1]{1,0:T(8,128)S(1)} %copy.11.ids_ref), custom_call_target="tpu_custom_call" | custom-call | tf_op jit(solution)/shard_map/pallas_call | solution.py:231
  23.0 45.9 %shard_map.68.refs_0_ = f32[1024,1024]{1,0:T(8,128)S(1)} custom-call(f32[128,1024]{1,0:T(8,128)S(1)} %bitcast.21), custom_call_target="tpu_custom_call" | custom-call | tf_op jit(solution)/shard_map/pallas_call | solution.py:289
  68.9 2.0 copy-done
  70.9 2.9 shard_map.69
  76.1 22.6 %shard_map.70 = (f32[128,512]{1,0:T(8,128)S(1)}, f32[8,128]{1,0:T(8,128)S(1)}, f32[512,512]{1,0:T(8,128)S(1)}) custom-call(s32[1]{0:T(128)} %bitcast.refs_0_, f32[512,1024]{1,0:T(8,128)S(1)} %get-tuple-element.40.refs_1_, f32[512,512]{1,0:T(8,128)S(1)} %copy-done.2, f32[8,128]{1,0:T(8,128)S(1)} %broadcast_in_dim.31.refs_3_), custom_call_target="tpu_custom_call" | custom-call | tf_op jit(solution)/shard_map/pallas_call | solution.py:147
  98.7 16.8 %shard_map.72 = (f32[512,512]{1,0:T(8,128)S(1)}, f32[8,128]{1,0:T(8,128)S(1)}) custom-call(f32[512,512]{1,0:T(8,128)S(1)} %get-tuple-element.43.upd_ref.refs_1_, f32[8,128]{1,0:T(8,128)S(1)} %get-tuple-element.44.log_ref), custom_call_target="tpu_custom_call" | custom-call | tf_op jit(solution)/shard_map/pallas_call | solution.py:365
  116.5 7.9 %shard_map.73 = (f32[512,1024]{1,0:T(8,128)S(1)}, f32[512,512]{1,0:T(8,128)S(1)}) custom-call(f32[1024,1024]{1,0:T(8,128)} %all-gather.7.cloned.1.call-done.refs_0_, f32[512,512]{1,0:T(8,128)S(1)} %get-tuple-element.43.upd_ref.refs_1_, s32[1,512]{1,0:T(1,128)S(1)} %get-tuple-element.90.refs_2_, f32[512,512]{1,0:T(8,128)S(1)} %get-tuple-element.45.refs_3_, ...), custom_call_target="tpu_custom_call" | custom-call | tf_op jit(solution)/shard_map/pallas_call | solution.py:203
  124.5 22.8 %shard_map.74 = (f32[64,512]{1,0:T(8,128)S(1)}, f32[8,128]{1,0:T(8,128)S(1)}, f32[512,512]{1,0:T(8,128)S(1)}) custom-call(s32[1]{0:T(128)} %bitcast.2.refs_0_, f32[512,1024]{1,0:T(8,128)S(1)} %get-tuple-element.46.refs_1_, f32[512,512]{1,0:T(8,128)S(1)} %get-tuple-element.47.refs_2_, f32[8,128]{1,0:T(8,128)S(1)} %add.160.refs_3_), custom_call_target="tpu_custom_call" | custom-call | tf_op jit(solution)/shard_map/pallas_call | solution.py:147
  147.3 20.2 %shard_map.75 = (f32[512,512]{1,0:T(8,128)S(1)}, f32[8,128]{1,0:T(8,128)S(1)}) custom-call(f32[512,512]{1,0:T(8,128)S(1)} %get-tuple-element.50.upd_ref.refs_1_, f32[8,128]{1,0:T(8,128)S(1)} %get-tuple-element.51.log_ref), custom_call_target="tpu_custom_call" | custom-call | tf_op jit(solution)/shard_map/pallas_call | solution.py:365
  167.6 7.9 %shard_map.76 = (f32[512,1024]{1,0:T(8,128)S(1)}, f32[512,512]{1,0:T(8,128)S(1)}) custom-call(f32[1024,1024]{1,0:T(8,128)} %all-gather.9.cloned.1.call-done.refs_0_, f32[512,512]{1,0:T(8,128)S(1)} %get-tuple-element.50.upd_ref.refs_1_, s32[1,512]{1,0:T(1,128)S(1)} %get-tuple-element.88.refs_2_, f32[512,512]{1,0:T(8,128)S(1)} %get-tuple-element.52.refs_3_, ...), custom_call_target="tpu_custom_call" | custom-call | tf_op jit(solution)/shard_map/pallas_call | solution.py:203
  175.5 23.0 %shard_map.77 = (f32[32,512]{1,0:T(8,128)S(1)}, f32[8,128]{1,0:T(8,128)S(1)}, f32[512,512]{1,0:T(8,128)S(1)}) custom-call(s32[1]{0:T(128)} %bitcast.6.refs_0_, f32[512,1024]{1,0:T(8,128)S(1)} %get-tuple-element.53.refs_1_, f32[512,512]{1,0:T(8,128)S(1)} %get-tuple-element.54.refs_2_, f32[8,128]{1,0:T(8,128)S(1)} %add.165.refs_3_), custom_call_target="tpu_custom_call" | custom-call | tf_op jit(solution)/shard_map/pallas_call | solution.py:147
  198.5 18.7 %shard_map.78 = (f32[512,512]{1,0:T(8,128)S(1)}, f32[8,128]{1,0:T(8,128)S(1)}) custom-call(f32[512,512]{1,0:T(8,128)S(1)} %get-tuple-element.57.upd_ref.refs_1_, f32[8,128]{1,0:T(8,128)S(1)} %get-tuple-element.58.log_ref), custom_call_target="tpu_custom_call" | custom-call | tf_op jit(solution)/shard_map/pallas_call | solution.py:365
  217.2 27.9 %all-gather.11.cloned.1.call-done.refs_0_ = f32[1024,1024]{1,0:T(8,128)} async-done(((f32[16,1024]{1,0:T(8,128)}), f32[1024,1024]{1,0:T(8,128)}) %all-gather.11.cloned.1.call-update) | async-done | bytes 4194320 | tf_op jit(solution)/shard_map/all_gather | solution.py:416
  245.1 7.9 %shard_map.79 = (f32[512,1024]{1,0:T(8,128)S(1)}, f32[512,512]{1,0:T(8,128)S(1)}) custom-call(f32[1024,1024]{1,0:T(8,128)} %all-gather.11.cloned.1.call-done.refs_0_, f32[512,512]{1,0:T(8,128)S(1)} %get-tuple-element.57.upd_ref.refs_1_, s32[1,512]{1,0:T(1,128)S(1)} %get-tuple-element.86.refs_2_, f32[512,512]{1,0:T(8,128)S(1)} %get-tuple-element.59.refs_3_, ...), custom_call_target="tpu_custom_call" | custom-call | tf_op jit(solution)/shard_map/pallas_call | solution.py:203
  253.0 22.8 %shard_map.80 = (f32[16,512]{1,0:T(8,128)S(1)}, f32[8,128]{1,0:T(8,128)S(1)}, f32[512,512]{1,0:T(8,128)S(1)}) custom-call(s32[1]{0:T(128)} %bitcast.7.refs_0_, f32[512,1024]{1,0:T(8,128)S(1)} %get-tuple-element.60.refs_1_, f32[512,512]{1,0:T(8,128)S(1)} %get-tuple-element.61.refs_2_, f32[8,128]{1,0:T(8,128)S(1)} %add.170.refs_3_), custom_call_target="tpu_custom_call" | custom-call | tf_op jit(solution)/shard_map/pallas_call | solution.py:147
  275.9 21.6 %shard_map.81 = (f32[512,512]{1,0:T(8,128)S(1)}, f32[8,128]{1,0:T(8,128)S(1)}) custom-call(f32[512,512]{1,0:T(8,128)S(1)} %get-tuple-element.64.upd_ref.refs_1_, f32[8,128]{1,0:T(8,128)S(1)} %get-tuple-element.65.log_ref), custom_call_target="tpu_custom_call" | custom-call | tf_op jit(solution)/shard_map/pallas_call | solution.py:365
  297.5 150.3 %all-gather.13.cloned.1.call-done.refs_0_ = f32[1024,1024]{1,0:T(8,128)} async-done(((f32[8,1024]{1,0:T(8,128)}), f32[1024,1024]{1,0:T(8,128)}) %all-gather.13.cloned.1.call-update) | async-done | bytes 4194320 | tf_op jit(solution)/shard_map/all_gather | solution.py:416
  447.8 7.9 %shard_map.82 = (f32[512,1024]{1,0:T(8,128)S(1)}, f32[512,512]{1,0:T(8,128)S(1)}) custom-call(f32[1024,1024]{1,0:T(8,128)} %all-gather.13.cloned.1.call-done.refs_0_, f32[512,512]{1,0:T(8,128)S(1)} %get-tuple-element.64.upd_ref.refs_1_, s32[1,512]{1,0:T(1,128)S(1)} %get-tuple-element.84.refs_2_, f32[512,512]{1,0:T(8,128)S(1)} %get-tuple-element.66.refs_3_, ...), custom_call_target="tpu_custom_call" | custom-call | tf_op jit(solution)/shard_map/pallas_call | solution.py:203
  455.7 22.8 %shard_map.83 = (f32[8,512]{1,0:T(8,128)S(1)}, f32[8,128]{1,0:T(8,128)S(1)}, f32[512,512]{1,0:T(8,128)S(1)}) custom-call(s32[1]{0:T(128)} %bitcast.8.refs_0_, f32[512,1024]{1,0:T(8,128)S(1)} %get-tuple-element.67.refs_1_, f32[512,512]{1,0:T(8,128)S(1)} %get-tuple-element.68.refs_2_, f32[8,128]{1,0:T(8,128)S(1)} %add.175.refs_3_), custom_call_target="tpu_custom_call" | custom-call | tf_op jit(solution)/shard_map/pallas_call | solution.py:147
  478.5 19.4 %shard_map.84 = (f32[512,512]{1,0:T(8,128)S(1)}, f32[8,128]{1,0:T(8,128)S(1)}) custom-call(f32[512,512]{1,0:T(8,128)S(1)} %get-tuple-element.71.upd_ref.refs_1_, f32[8,128]{1,0:T(8,128)S(1)} %get-tuple-element.72.log_ref), custom_call_target="tpu_custom_call" | custom-call | tf_op jit(solution)/shard_map/pallas_call | solution.py:365
  497.9 68.4 %all-gather.15.cloned.1.call-done = f32[256,4,1024]{2,1,0:T(4,128)} async-done(((f32[1,4,1024]{2,1,0:T(4,128)}), f32[256,4,1024]{2,1,0:T(4,128)}) %all-gather.15.cloned.1.call-update) | async-done | bytes 4194320 | tf_op jit(solution)/shard_map/all_gather | solution.py:418
  566.4 5.4 reshape.5.refs_0_
  571.8 8.9 %shard_map.85 = (f32[512,1024]{1,0:T(8,128)S(1)}, f32[512,512]{1,0:T(8,128)}) custom-call(f32[1024,1024]{1,0:T(8,128)} %reshape.5.refs_0_, f32[512,512]{1,0:T(8,128)S(1)} %get-tuple-element.71.upd_ref.refs_1_, s32[1,512]{1,0:T(1,128)S(1)} %get-tuple-element.91.refs_2_, f32[512,512]{1,0:T(8,128)S(1)} %get-tuple-element.73.refs_3_, ...), custom_call_target="tpu_custom_call" | custom-call | tf_op jit(solution)/shard_map/pallas_call | solution.py:203
  580.6 22.0 %shard_map.86 = (f32[4,512]{1,0:T(4,128)S(1)}, f32[8,128]{1,0:T(8,128)S(1)}) custom-call(s32[1]{0:T(128)} %bitcast.9.refs_0_, f32[512,1024]{1,0:T(8,128)S(1)} %get-tuple-element.74.refs_1_, f32[8,128]{1,0:T(8,128)S(1)} %add.180.refs_2_), custom_call_target="tpu_custom_call" | custom-call | tf_op jit(solution)/shard_map/pallas_call | solution.py:147
  (53 shorter events, 12.5 us)
Async XLA Ops:
  7.2 109.4 %all-gather.7.cloned.1.call-start = ((), (), s32[]{:S(2)}) async-start(), calls=%async_computation | async-start | bytes 4456448 | tf_op jit(solution)/shard_map/all_gather | solution.py:416
  19.1 148.5 %all-gather.9.cloned.1.call-start = ((), (), s32[]{:S(2)}) async-start(), calls=%async_computation.1 | async-start | bytes 4325376 | tf_op jit(solution)/shard_map/all_gather | solution.py:416
  19.8 225.3 %all-gather.11.cloned.1.call-start = ((), (), s32[]{:S(2)}) async-start(), calls=%async_computation.2 | async-start | bytes 4259840 | tf_op jit(solution)/shard_map/all_gather | solution.py:416
  20.6 427.2 %all-gather.13.cloned.1.call-start = ((), (), s32[]{:S(2)}) async-start(), calls=%async_computation.3 | async-start | bytes 4227072 | tf_op jit(solution)/shard_map/all_gather | solution.py:416
  21.3 545.1 %all-gather.15.cloned.1.call-start = ((), (), s32[]{:S(2)}) async-start(), calls=%async_computation.4 | async-start | bytes 4210688 | tf_op jit(solution)/shard_map/all_gather | solution.py:418
  22.0 1.0 copy-start.3
  68.9 2.0 copy-start
  73.8 1.0 copy-start.1
  74.8 1.2 copy-start.2
Sparse Core Ops, SparseCore 0:
  19.2 54.1 all-gather.6
  76.0 55.0 all-gather.8
  132.9 112.1 all-gather.10
  246.9 200.8 all-gather.12
  451.2 115.1 all-gather.14
